TPU v7x, 512 devices: a whole 4x4x16 slice. The times are simulated.
512 devices in a mesh: face: 8 (over x, y_lo), tile: 64 (over z, y_hi, core).
Axes of the slice: x: 4, y: 4 (y_hi: 2, y_lo: 2; y = y_hi * 2 + y_lo), z: 16, core: 2. Of those that a mesh axis runs over, the one named last changes fastest.
Arguments:
- maps: bfloat16 [4, 4, 128, 8192], P(None, None, 'face', 'tile'), may hold values from -8 to 8
- params: float32 [4, 2], replicated, may hold values from 0 to 1
- labels: int32 [4], replicated, may hold values 0 or 1
- edge_flip: int32 [8, 64], replicated, may hold values from 0 to 1
- fine_weight: float32 [3, 4, 16], replicated, may hold values from -1.75 to 1.75
- coarse_weight: float32 [3, 16, 32], replicated, may hold values from -0.875 to 0.875
- feature_weight: float32 [32, 128], replicated, may hold values from -2 to 2
- param_weight: float32 [2, 128], replicated, may hold values from -4 to 4
- out_weight: float32 [128], replicated, may hold values from -1 to 1
Outputs:
- logits: float32 [4], replicated
- saliency: float32 [4, 4, 128, 8192], P(None, None, 'face', 'tile')
- grad_fine: float32 [3, 4, 16], replicated
- grad_coarse: float32 [3, 16, 32], replicated
All inputs are finite; a program needn't handle non-finite values.
Results may differ from a plain program's by a relative error of at most 0.0003.
Values sent between devices are 32-bit elements; how exact they have to be, the bound alone decides.
No kernel may reach another device: no remote copies, remote signals or barrier semaphores. Data moves between devices by JAX's collectives and lax.ppermute only.
A program may use at most 64 MiB of HBM per device.

v0:
```python
import jax
import jax.numpy as jnp
from jax import lax
from jax.sharding import PartitionSpec as P

exact = lax.Precision.HIGHEST


def with_halo(block, sides, width):
    for axis, dim in sides:
        count = lax.axis_size(axis)
        forward = [(i, i + 1) for i in range(count - 1)]
        forward.append((count - 1, 0))
        backward = [(target, source) for source, target in forward]
        low = lax.ppermute(
            lax.slice_in_dim(block, block.shape[dim] - width, None, axis=dim), axis, forward
        )
        high = lax.ppermute(lax.slice_in_dim(block, 0, width, axis=dim), axis, backward)
        block = jnp.concatenate([low, block, high], axis=dim)
    return block


def turn_blocks(edge_row, width):
    lead = edge_row.shape[:-1]
    return edge_row.reshape(lead + (-1, width))[..., ::-1].reshape(edge_row.shape)


def face_flags(edge_flip):
    position = lax.axis_index("face")
    faces = edge_flip.shape[0]
    return (edge_flip[position] == 1, edge_flip[(position + 1) % faces] == 1)


def tile_flags(flags):
    tiles = flags[0].shape[0]
    spot = lax.axis_index("tile") % tiles
    return (flags[0][spot], flags[1][spot])


def stencil(padded, flags, width):
    top_flag, bottom_flag = tile_flags(flags)
    left = padded[..., 1:-1, :-2]
    right = padded[..., 1:-1, 2:]
    upper = padded[..., :-2, 1:-1]
    lower = padded[..., 2:, 1:-1]
    top_row = upper[..., 0, :]
    upper = upper.at[..., 0, :].set(jnp.where(top_flag, turn_blocks(top_row, width), top_row))
    bottom_row = lower[..., -1, :]
    lower = lower.at[..., -1, :].set(
        jnp.where(bottom_flag, turn_blocks(bottom_row, width), bottom_row)
    )
    return -0.25 * (upper + lower + left + right)


def fine_apply(field, flags):
    padded = with_halo(field, (("face", 2), ("tile", 3)), 1)
    return stencil(padded, flags, field.shape[-1])


def coarse_apply(field, flags):
    padded = with_halo(field, (("face", 2), ("tile", 3)), 1)
    return stencil(padded, flags, field.shape[-1])


def coarse_terms(field, flags):
    first = coarse_apply(field, flags)
    second = 2.0 * coarse_apply(first, flags) - field
    return (first, second)


def coarse_adjoint(parts, flags):
    inner = coarse_apply(parts[2], flags)
    outer = coarse_apply(parts[1] + 2.0 * inner, flags)
    return parts[0] - parts[2] + outer


def on_device(
    maps,
    params,
    labels,
    edge_flip,
    fine_weight,
    coarse_weight,
    feature_weight,
    param_weight,
    out_weight,
):
    flags = face_flags(edge_flip)
    field0 = maps.astype(jnp.float32)
    first0 = fine_apply(field0, flags)
    second0 = 2.0 * fine_apply(first0, flags) - field0
    terms0 = jnp.stack([field0, first0, second0])
    pre0 = jnp.einsum("kio,kbirc->borc", fine_weight, terms0, precision=exact)
    act0 = jax.nn.softplus(pre0)
    nmaps, nchan, nrows, ncols = act0.shape
    field1 = act0.reshape(nmaps, nchan, nrows // 2, 2, ncols // 2, 2).mean(axis=(3, 5))
    first1, second1 = coarse_terms(field1, flags)
    terms1 = jnp.stack([field1, first1, second1])
    pre1 = jnp.einsum("kio,kbirc->borc", coarse_weight, terms1, precision=exact)
    act1 = jax.nn.softplus(pre1)
    pooled_count = nrows // 2 * lax.axis_size("face") * (ncols // 2) * lax.axis_size("tile")
    features = lax.psum(act1.sum(axis=(2, 3)), ("face", "tile")) / pooled_count
    hidden = jnp.tanh(
        jnp.dot(features, feature_weight, precision=exact)
        + jnp.dot(params, param_weight, precision=exact)
    )
    logits = jnp.dot(hidden, out_weight, precision=exact)
    dlogit = jax.nn.sigmoid(logits) - labels.astype(jnp.float32)
    dhidden = dlogit[:, None] * out_weight[None, :] * (1.0 - hidden * hidden)
    dfeatures = jnp.dot(dhidden, feature_weight.T, precision=exact)
    dpre1 = (dfeatures / pooled_count)[:, :, None, None] * jax.nn.sigmoid(pre1)
    grad_c = jnp.einsum("kbirc,borc->kio", terms1, dpre1, precision=exact)
    parts1 = jnp.einsum("kio,borc->kbirc", coarse_weight, dpre1, precision=exact)
    dfield1 = coarse_adjoint(parts1, flags)
    spread = jnp.broadcast_to(
        dfield1[:, :, :, None, :, None], (nmaps, nchan, nrows // 2, 2, ncols // 2, 2)
    ).reshape(pre0.shape)
    dpre0 = 0.25 * spread * jax.nn.sigmoid(pre0)
    grad_f = jnp.einsum("kbirc,borc->kio", terms0, dpre0, precision=exact)
    parts0 = jnp.einsum("kio,borc->kbirc", fine_weight, dpre0, precision=exact)
    inner0 = fine_apply(parts0[2], flags)
    outer0 = fine_apply(parts0[1] + 2.0 * inner0, flags)
    pixel_count = nrows * lax.axis_size("face") * ncols * lax.axis_size("tile")
    saliency = (parts0[0] - parts0[2] + outer0) * pixel_count
    grad_f, grad_c = lax.psum((grad_f, grad_c), ("face", "tile"))
    return (logits, saliency, grad_f, grad_c)


def solution(mesh):
    in_specs = (P(None, None, "face", "tile"), P(), P(), P(), P(), P(), P(), P(), P())
    out_specs = (P(), P(None, None, "face", "tile"), P(), P())
    return jax.shard_map(
        on_device, mesh=mesh, in_specs=in_specs, out_specs=out_specs, check_vma=False
    )
```

profile of v0, /device:TPU:1, one launch (start us, length us, event | category | flops | bytes accessed | tf_op | source)
XLA Modules:
  0.0 429.5 jit_solution(592526183360856192)
XLA Ops:
  5.6 4.1 collective-permute-start.1
  12.0 6.0 %collective-permute-start.2 = (f32[4,4,18,1]{3,1,2,0:T(4,128)S(1)}, f32[4,4,18,1]{3,1,2,0:T(4,128)S(1)}, u32[]{:S(2)}, u32[]{:S(2)}) collective-permute-start(f32[4,4,18,1]{3,1,2,0:T(4,128)S(1)} %get-tuple-element.242), channel_id=1, source_target_pairs={{0,1},{1,2},{2,3},{3,4},{4,5},{5,6},{6,7},{7,8},{8,9},{9,10},{10,1... | collective-permute-start | bytes 3464 | tf_op jit(solution)/shard_map/ppermute | solution.py:15
  18.1 4.5 %collective-permute-start.3 = (f32[4,4,18,1]{3,1,2,0:T(4,128)S(1)}, f32[4,4,18,1]{3,1,2,0:T(4,128)S(1)}, u32[]{:S(2)}, u32[]{:S(2)}) collective-permute-start(f32[4,4,18,1]{3,1,2,0:T(4,128)S(1)} %get-tuple-element.243), channel_id=1, source_target_pairs={{1,0},{2,1},{3,2},{4,3},{5,4},{6,5},{7,6},{8,7},{9,8},{10,9},{11,1... | collective-permute-start | bytes 3464 | tf_op jit(solution)/shard_map/ppermute | solution.py:18
  28.9 4.8 %collective-permute-start.5 = (f32[4,4,1,128]{3,1,2,0:T(4,128)S(1)}, f32[4,4,1,128]{3,1,2,0:T(4,128)S(1)}, u32[]{:S(2)}, u32[]{:S(2)}) collective-permute-start(f32[4,4,1,128]{3,1,2,0:T(4,128)S(1)} %get-tuple-element.255), channel_id=1, source_target_pairs={{64,0},{128,64},{192,128},{256,192},{320,256},{384,320},{448,384},... | collective-permute-start | bytes 24584 | tf_op jit(solution)/shard_map/ppermute | solution.py:18
  37.6 6.9 %collective-permute-start.7 = (f32[4,4,18,1]{3,1,2,0:T(4,128)S(1)}, f32[4,4,18,1]{3,1,2,0:T(4,128)S(1)}, u32[]{:S(2)}, u32[]{:S(2)}) collective-permute-start(f32[4,4,18,1]{3,1,2,0:T(4,128)S(1)} %get-tuple-element.241), channel_id=1, source_target_pairs={{1,0},{2,1},{3,2},{4,3},{5,4},{6,5},{7,6},{8,7},{9,8},{10,9},{11,1... | collective-permute-start | bytes 3464 | tf_op jit(solution)/shard_map/ppermute | solution.py:18
  51.6 5.6 %reduce_sum.18 = f32[4,16,8,64]{1,3,2,0:T(8,128)S(1)} reduce(f32[4,16,8,2,64,2]{1,5,4,3,2,0:T(2,128)} %bitcast.121, f32[]{:T(128)} %constant.422.clone.1), dimensions={3,5}, to_apply=%region_0.1 | reduce | flops 98304 | bytes 655364 | tf_op jit(solution)/shard_map/reduce_sum | solution.py:96
  60.1 5.4 %collective-permute-start.9 = (f32[4,16,1,64]{3,1,2,0:T(8,128)S(1)}, f32[4,16,1,64]{3,1,2,0:T(8,128)S(1)}, u32[]{:S(2)}, u32[]{:S(2)}) collective-permute-start(f32[4,16,1,64]{3,1,2,0:T(8,128)S(1)} %get-tuple-element.235), channel_id=1, source_target_pairs={{64,0},{128,64},{192,128},{256,192},{320,256},{384,320},{448,384},... | collective-permute-start | bytes 49160 | tf_op jit(solution)/shard_map/ppermute | solution.py:18
  68.8 9.0 %collective-permute-start.11 = (f32[4,16,10,1]{3,1,2,0:T(8,128)S(1)}, f32[4,16,10,1]{3,1,2,0:T(8,128)S(1)}, u32[]{:S(2)}, u32[]{:S(2)}) collective-permute-start(f32[4,16,10,1]{3,1,2,0:T(8,128)S(1)} %get-tuple-element.217), channel_id=1, source_target_pairs={{1,0},{2,1},{3,2},{4,3},{5,4},{6,5},{7,6},{8,7},{9,8},{10,9},{11,1... | collective-permute-start | bytes 7688 | tf_op jit(solution)/shard_map/ppermute | solution.py:18
  81.7 6.2 %collective-permute-start.13 = (f32[4,16,1,64]{3,1,2,0:T(8,128)S(1)}, f32[4,16,1,64]{3,1,2,0:T(8,128)S(1)}, u32[]{:S(2)}, u32[]{:S(2)}) collective-permute-start(f32[4,16,1,64]{3,1,2,0:T(8,128)S(1)} %get-tuple-element.231), channel_id=1, source_target_pairs={{64,0},{128,64},{192,128},{256,192},{320,256},{384,320},{448,384},... | collective-permute-start | bytes 49160 | tf_op jit(solution)/shard_map/ppermute | solution.py:18
  91.0 11.0 %collective-permute-start.15 = (f32[4,16,10,1]{3,1,2,0:T(8,128)S(1)}, f32[4,16,10,1]{3,1,2,0:T(8,128)S(1)}, u32[]{:S(2)}, u32[]{:S(2)}) collective-permute-start(f32[4,16,10,1]{3,1,2,0:T(8,128)S(1)} %get-tuple-element.215), channel_id=1, source_target_pairs={{1,0},{2,1},{3,2},{4,3},{5,4},{6,5},{7,6},{8,7},{9,8},{10,9},{11,1... | collective-permute-start | bytes 7688 | tf_op jit(solution)/shard_map/ppermute | solution.py:18
  105.7 115.2 %psum.21 = f32[4,32]{1,0:T(4,128)S(1)} all-reduce(f32[4,32]{1,0:T(4,128)S(1)} %get-tuple-element.266), channel_id=1, replica_groups=mesh['face'=8,'tile'=64] {'face','tile'}, use_global_device_ids=true, to_apply=%region_2.3 | all-reduce | flops 128 | bytes 1024 | tf_op jit(solution)/shard_map/psum | solution.py:102
  225.0 5.5 %collective-permute-start.17 = (f32[4,16,1,64]{3,1,2,0:T(8,128)S(1)}, f32[4,16,1,64]{3,1,2,0:T(8,128)S(1)}, u32[]{:S(2)}, u32[]{:S(2)}) collective-permute-start(f32[4,16,1,64]{3,1,2,0:T(8,128)S(1)} %get-tuple-element.225), channel_id=1, source_target_pairs={{64,0},{128,64},{192,128},{256,192},{320,256},{384,320},{448,384},... | collective-permute-start | bytes 49160 | tf_op jit(solution)/shard_map/ppermute | solution.py:18
  232.4 4.7 %collective-permute-start.18 = (f32[4,16,10,1]{3,1,2,0:T(8,128)}, f32[4,16,10,1]{3,1,2,0:T(8,128)S(1)}, u32[]{:S(2)}, u32[]{:S(2)}) collective-permute-start(f32[4,16,10,1]{3,1,2,0:T(8,128)} %get-tuple-element.212), channel_id=1, source_target_pairs={{0,1},{1,2},{2,3},{3,4},{4,5},{5,6},{6,7},{7,8},{8,9},{9,10},{10,1... | collective-permute-start | bytes 7688 | tf_op jit(solution)/shard_map/ppermute | solution.py:15
  241.4 8.2 %collective-permute-done.19 = f32[4,16,10,1]{3,1,2,0:T(8,128)S(1)} collective-permute-done((f32[4,16,10,1]{3,1,2,0:T(8,128)S(1)}, f32[4,16,10,1]{3,1,2,0:T(8,128)S(1)}, u32[]{:S(2)}, u32[]{:S(2)}) %collective-permute-start.19) | collective-permute-done | bytes 2592 | tf_op jit(solution)/shard_map/ppermute | solution.py:18
  251.8 6.1 %collective-permute-start.21 = (f32[4,16,1,64]{3,1,2,0:T(8,128)S(1)}, f32[4,16,1,64]{3,1,2,0:T(8,128)S(1)}, u32[]{:S(2)}, u32[]{:S(2)}) collective-permute-start(f32[4,16,1,64]{3,1,2,0:T(8,128)S(1)} %get-tuple-element.221), channel_id=1, source_target_pairs={{64,0},{128,64},{192,128},{256,192},{320,256},{384,320},{448,384},... | collective-permute-start | bytes 49160 | tf_op jit(solution)/shard_map/ppermute | solution.py:18
  266.6 4.3 %collective-permute-done.22 = f32[4,16,10,1]{3,1,2,0:T(8,128)S(1)} collective-permute-done((f32[4,16,10,1]{3,1,2,0:T(8,128)}, f32[4,16,10,1]{3,1,2,0:T(8,128)S(1)}, u32[]{:S(2)}, u32[]{:S(2)}) %collective-permute-start.22) | collective-permute-done | bytes 2592 | tf_op jit(solution)/shard_map/ppermute | solution.py:15
  271.0 4.1 collective-permute-done.23
  275.7 4.0 broadcast_in_dim.2
  285.4 5.5 %collective-permute-start.25 = (f32[4,4,1,128]{3,1,2,0:T(4,128)S(1)}, f32[4,4,1,128]{3,1,2,0:T(4,128)S(1)}, u32[]{:S(2)}, u32[]{:S(2)}) collective-permute-start(f32[4,4,1,128]{3,1,2,0:T(4,128)S(1)} %get-tuple-element.251), channel_id=1, source_target_pairs={{64,0},{128,64},{192,128},{256,192},{320,256},{384,320},{448,384},... | collective-permute-start | bytes 24584 | tf_op jit(solution)/shard_map/ppermute | solution.py:18
  298.7 4.3 %collective-permute-done.27 = f32[4,4,18,1]{3,1,2,0:T(4,128)S(1)} collective-permute-done((f32[4,4,18,1]{3,1,2,0:T(4,128)S(1)}, f32[4,4,18,1]{3,1,2,0:T(4,128)S(1)}, u32[]{:S(2)}, u32[]{:S(2)}) %collective-permute-start.27) | collective-permute-done | bytes 1184 | tf_op jit(solution)/shard_map/ppermute | solution.py:18
  305.2 5.7 %collective-permute-start.29 = (f32[4,4,1,128]{3,1,2,0:T(4,128)S(1)}, f32[4,4,1,128]{3,1,2,0:T(4,128)S(1)}, u32[]{:S(2)}, u32[]{:S(2)}) collective-permute-start(f32[4,4,1,128]{3,1,2,0:T(4,128)S(1)} %get-tuple-element.247), channel_id=1, source_target_pairs={{64,0},{128,64},{192,128},{256,192},{320,256},{384,320},{448,384},... | collective-permute-start | bytes 24584 | tf_op jit(solution)/shard_map/ppermute | solution.py:18
  312.6 103.5 %all-reduce = (f32[3,4,16]{2,1,0:T(4,128)}, f32[3,16,32]{2,1,0:T(8,128)}) all-reduce(f32[3,4,16]{2,1,0:T(4,128)S(1)} %convolution_bitcast_fusion.5, f32[3,16,32]{2,1,0:T(8,128)S(1)} %convolution_bitcast_fusion.4), channel_id=1, replica_groups=mesh['face'=8,'tile'=64] {'face','tile'}, use_global_device_ids=true, to_apply=%region_3.4 | all-reduce | flops 1728 | bytes 13824 | tf_op jit(solution)/shard_map/psum | solution.py:125
  416.4 4.2 collective-permute-start.30
  424.1 4.4 %collective-permute-done.31 = f32[4,4,18,1]{3,1,2,0:T(4,128)S(1)} collective-permute-done((f32[4,4,18,1]{3,1,2,0:T(4,128)S(1)}, f32[4,4,18,1]{3,1,2,0:T(4,128)S(1)}, u32[]{:S(2)}, u32[]{:S(2)}) %collective-permute-start.31) | collective-permute-done | bytes 1184 | tf_op jit(solution)/shard_map/ppermute | solution.py:18
  (169 shorter events, 84.6 us)
Async XLA Ops:
  1.6 10.3 %collective-permute-start = (f32[4,4,1,128]{3,1,2,0:T(4,128)S(1)}, f32[4,4,1,128]{3,1,2,0:T(4,128)S(1)}, u32[]{:S(2)}, u32[]{:S(2)}) collective-permute-start(f32[4,4,1,128]{3,1,2,0:T(4,128)S(1)} %get-tuple-element.258), channel_id=1, source_target_pairs={{0,64},{64,128},{128,192},{192,256},{256,320},{320,384},{384,448},... | collective-permute-start | bytes 24584 | tf_op jit(solution)/shard_map/ppermute | solution.py:15
  12.0 12.1 %collective-permute-start.2 = (f32[4,4,18,1]{3,1,2,0:T(4,128)S(1)}, f32[4,4,18,1]{3,1,2,0:T(4,128)S(1)}, u32[]{:S(2)}, u32[]{:S(2)}) collective-permute-start(f32[4,4,18,1]{3,1,2,0:T(4,128)S(1)} %get-tuple-element.242), channel_id=1, source_target_pairs={{0,1},{1,2},{2,3},{3,4},{4,5},{5,6},{6,7},{7,8},{8,9},{9,10},{10,1... | collective-permute-start | bytes 3464 | tf_op jit(solution)/shard_map/ppermute | solution.py:15
  18.1 8.0 %collective-permute-start.3 = (f32[4,4,18,1]{3,1,2,0:T(4,128)S(1)}, f32[4,4,18,1]{3,1,2,0:T(4,128)S(1)}, u32[]{:S(2)}, u32[]{:S(2)}) collective-permute-start(f32[4,4,18,1]{3,1,2,0:T(4,128)S(1)} %get-tuple-element.243), channel_id=1, source_target_pairs={{1,0},{2,1},{3,2},{4,3},{5,4},{6,5},{7,6},{8,7},{9,8},{10,9},{11,1... | collective-permute-start | bytes 3464 | tf_op jit(solution)/shard_map/ppermute | solution.py:18
  26.3 7.4 %collective-permute-start.4 = (f32[4,4,1,128]{3,1,2,0:T(4,128)S(1)}, f32[4,4,1,128]{3,1,2,0:T(4,128)S(1)}, u32[]{:S(2)}, u32[]{:S(2)}) collective-permute-start(f32[4,4,1,128]{3,1,2,0:T(4,128)S(1)} %get-tuple-element.254), channel_id=1, source_target_pairs={{0,64},{64,128},{128,192},{192,256},{256,320},{320,384},{384,448},... | collective-permute-start | bytes 24584 | tf_op jit(solution)/shard_map/ppermute | solution.py:15
  34.7 11.4 %collective-permute-start.6 = (f32[4,4,18,1]{3,1,2,0:T(4,128)S(1)}, f32[4,4,18,1]{3,1,2,0:T(4,128)S(1)}, u32[]{:S(2)}, u32[]{:S(2)}) collective-permute-start(f32[4,4,18,1]{3,1,2,0:T(4,128)S(1)} %get-tuple-element.240), channel_id=1, source_target_pairs={{0,1},{1,2},{2,3},{3,4},{4,5},{5,6},{6,7},{7,8},{8,9},{9,10},{10,1... | collective-permute-start | bytes 3464 | tf_op jit(solution)/shard_map/ppermute | solution.py:15
  37.6 8.5 %collective-permute-start.7 = (f32[4,4,18,1]{3,1,2,0:T(4,128)S(1)}, f32[4,4,18,1]{3,1,2,0:T(4,128)S(1)}, u32[]{:S(2)}, u32[]{:S(2)}) collective-permute-start(f32[4,4,18,1]{3,1,2,0:T(4,128)S(1)} %get-tuple-element.241), channel_id=1, source_target_pairs={{1,0},{2,1},{3,2},{4,3},{5,4},{6,5},{7,6},{8,7},{9,8},{10,9},{11,1... | collective-permute-start | bytes 3464 | tf_op jit(solution)/shard_map/ppermute | solution.py:18
  57.6 8.0 %collective-permute-start.8 = (f32[4,16,1,64]{3,1,2,0:T(8,128)S(1)}, f32[4,16,1,64]{3,1,2,0:T(8,128)S(1)}, u32[]{:S(2)}, u32[]{:S(2)}) collective-permute-start(f32[4,16,1,64]{3,1,2,0:T(8,128)S(1)} %get-tuple-element.234), channel_id=1, source_target_pairs={{0,64},{64,128},{128,192},{192,256},{256,320},{320,384},{384,448},... | collective-permute-start | bytes 49160 | tf_op jit(solution)/shard_map/ppermute | solution.py:15
  66.8 12.6 %collective-permute-start.10 = (f32[4,16,10,1]{3,1,2,0:T(8,128)S(1)}, f32[4,16,10,1]{3,1,2,0:T(8,128)S(1)}, u32[]{:S(2)}, u32[]{:S(2)}) collective-permute-start(f32[4,16,10,1]{3,1,2,0:T(8,128)S(1)} %get-tuple-element.216), channel_id=1, source_target_pairs={{0,1},{1,2},{2,3},{3,4},{4,5},{5,6},{6,7},{7,8},{8,9},{9,10},{10,1... | collective-permute-start | bytes 7688 | tf_op jit(solution)/shard_map/ppermute | solution.py:15
  68.8 10.6 %collective-permute-start.11 = (f32[4,16,10,1]{3,1,2,0:T(8,128)S(1)}, f32[4,16,10,1]{3,1,2,0:T(8,128)S(1)}, u32[]{:S(2)}, u32[]{:S(2)}) collective-permute-start(f32[4,16,10,1]{3,1,2,0:T(8,128)S(1)} %get-tuple-element.217), channel_id=1, source_target_pairs={{1,0},{2,1},{3,2},{4,3},{5,4},{6,5},{7,6},{8,7},{9,8},{10,9},{11,1... | collective-permute-start | bytes 7688 | tf_op jit(solution)/shard_map/ppermute | solution.py:18
  79.8 8.1 %collective-permute-start.12 = (f32[4,16,1,64]{3,1,2,0:T(8,128)S(1)}, f32[4,16,1,64]{3,1,2,0:T(8,128)S(1)}, u32[]{:S(2)}, u32[]{:S(2)}) collective-permute-start(f32[4,16,1,64]{3,1,2,0:T(8,128)S(1)} %get-tuple-element.230), channel_id=1, source_target_pairs={{0,64},{64,128},{128,192},{192,256},{256,320},{320,384},{384,448},... | collective-permute-start | bytes 49160 | tf_op jit(solution)/shard_map/ppermute | solution.py:15
  89.1 14.6 %collective-permute-start.14 = (f32[4,16,10,1]{3,1,2,0:T(8,128)S(1)}, f32[4,16,10,1]{3,1,2,0:T(8,128)S(1)}, u32[]{:S(2)}, u32[]{:S(2)}) collective-permute-start(f32[4,16,10,1]{3,1,2,0:T(8,128)S(1)} %get-tuple-element.214), channel_id=1, source_target_pairs={{0,1},{1,2},{2,3},{3,4},{4,5},{5,6},{6,7},{7,8},{8,9},{9,10},{10,1... | collective-permute-start | bytes 7688 | tf_op jit(solution)/shard_map/ppermute | solution.py:15
  91.0 12.6 %collective-permute-start.15 = (f32[4,16,10,1]{3,1,2,0:T(8,128)S(1)}, f32[4,16,10,1]{3,1,2,0:T(8,128)S(1)}, u32[]{:S(2)}, u32[]{:S(2)}) collective-permute-start(f32[4,16,10,1]{3,1,2,0:T(8,128)S(1)} %get-tuple-element.215), channel_id=1, source_target_pairs={{1,0},{2,1},{3,2},{4,3},{5,4},{6,5},{7,6},{8,7},{9,8},{10,9},{11,1... | collective-permute-start | bytes 7688 | tf_op jit(solution)/shard_map/ppermute | solution.py:18
  223.1 7.4 %collective-permute-start.16 = (f32[4,16,1,64]{3,1,2,0:T(8,128)S(1)}, f32[4,16,1,64]{3,1,2,0:T(8,128)S(1)}, u32[]{:S(2)}, u32[]{:S(2)}) collective-permute-start(f32[4,16,1,64]{3,1,2,0:T(8,128)S(1)} %get-tuple-element.224), channel_id=1, source_target_pairs={{0,64},{64,128},{128,192},{192,256},{256,320},{320,384},{384,448},... | collective-permute-start | bytes 49160 | tf_op jit(solution)/shard_map/ppermute | solution.py:15
  232.4 9.0 %collective-permute-start.18 = (f32[4,16,10,1]{3,1,2,0:T(8,128)}, f32[4,16,10,1]{3,1,2,0:T(8,128)S(1)}, u32[]{:S(2)}, u32[]{:S(2)}) collective-permute-start(f32[4,16,10,1]{3,1,2,0:T(8,128)} %get-tuple-element.212), channel_id=1, source_target_pairs={{0,1},{1,2},{2,3},{3,4},{4,5},{5,6},{6,7},{7,8},{8,9},{9,10},{10,1... | collective-permute-start | bytes 7688 | tf_op jit(solution)/shard_map/ppermute | solution.py:15
  237.1 12.5 %collective-permute-start.19 = (f32[4,16,10,1]{3,1,2,0:T(8,128)S(1)}, f32[4,16,10,1]{3,1,2,0:T(8,128)S(1)}, u32[]{:S(2)}, u32[]{:S(2)}) collective-permute-start(f32[4,16,10,1]{3,1,2,0:T(8,128)S(1)} %get-tuple-element.213), channel_id=1, source_target_pairs={{1,0},{2,1},{3,2},{4,3},{5,4},{6,5},{7,6},{8,7},{9,8},{10,9},{11,1... | collective-permute-start | bytes 7688 | tf_op jit(solution)/shard_map/ppermute | solution.py:18
  249.9 8.0 %collective-permute-start.20 = (f32[4,16,1,64]{3,1,2,0:T(8,128)S(1)}, f32[4,16,1,64]{3,1,2,0:T(8,128)S(1)}, u32[]{:S(2)}, u32[]{:S(2)}) collective-permute-start(f32[4,16,1,64]{3,1,2,0:T(8,128)S(1)} %get-tuple-element.220), channel_id=1, source_target_pairs={{0,64},{64,128},{128,192},{192,256},{256,320},{320,384},{384,448},... | collective-permute-start | bytes 49160 | tf_op jit(solution)/shard_map/ppermute | solution.py:15
  259.8 11.1 %collective-permute-start.22 = (f32[4,16,10,1]{3,1,2,0:T(8,128)}, f32[4,16,10,1]{3,1,2,0:T(8,128)S(1)}, u32[]{:S(2)}, u32[]{:S(2)}) collective-permute-start(f32[4,16,10,1]{3,1,2,0:T(8,128)} %get-tuple-element.210), channel_id=1, source_target_pairs={{0,1},{1,2},{2,3},{3,4},{4,5},{5,6},{6,7},{7,8},{8,9},{9,10},{10,1... | collective-permute-start | bytes 7688 | tf_op jit(solution)/shard_map/ppermute | solution.py:15
  263.1 11.9 %collective-permute-start.23 = (f32[4,16,10,1]{3,1,2,0:T(8,128)S(1)}, f32[4,16,10,1]{3,1,2,0:T(8,128)S(1)}, u32[]{:S(2)}, u32[]{:S(2)}) collective-permute-start(f32[4,16,10,1]{3,1,2,0:T(8,128)S(1)} %get-tuple-element.211), channel_id=1, source_target_pairs={{1,0},{2,1},{3,2},{4,3},{5,4},{6,5},{7,6},{8,7},{9,8},{10,9},{11,1... | collective-permute-start | bytes 7688 | tf_op jit(solution)/shard_map/ppermute | solution.py:18
  283.5 8.3 %collective-permute-start.24 = (f32[4,4,1,128]{3,1,2,0:T(4,128)S(1)}, f32[4,4,1,128]{3,1,2,0:T(4,128)S(1)}, u32[]{:S(2)}, u32[]{:S(2)}) collective-permute-start(f32[4,4,1,128]{3,1,2,0:T(4,128)S(1)} %get-tuple-element.250), channel_id=1, source_target_pairs={{0,64},{64,128},{128,192},{192,256},{256,320},{320,384},{384,448},... | collective-permute-start | bytes 24584 | tf_op jit(solution)/shard_map/ppermute | solution.py:15
  295.1 8.0 %collective-permute-start.27 = (f32[4,4,18,1]{3,1,2,0:T(4,128)S(1)}, f32[4,4,18,1]{3,1,2,0:T(4,128)S(1)}, u32[]{:S(2)}, u32[]{:S(2)}) collective-permute-start(f32[4,4,18,1]{3,1,2,0:T(4,128)S(1)} %get-tuple-element.239), channel_id=1, source_target_pairs={{1,0},{2,1},{3,2},{4,3},{5,4},{6,5},{7,6},{8,7},{9,8},{10,9},{11,1... | collective-permute-start | bytes 3464 | tf_op jit(solution)/shard_map/ppermute | solution.py:18
  303.3 112.9 %collective-permute-start.28 = (f32[4,4,1,128]{3,1,2,0:T(4,128)S(1)}, f32[4,4,1,128]{3,1,2,0:T(4,128)S(1)}, u32[]{:S(2)}, u32[]{:S(2)}) collective-permute-start(f32[4,4,1,128]{3,1,2,0:T(4,128)S(1)} %get-tuple-element.246), channel_id=1, source_target_pairs={{0,64},{64,128},{128,192},{192,256},{256,320},{320,384},{384,448},... | collective-permute-start | bytes 24584 | tf_op jit(solution)/shard_map/ppermute | solution.py:15
  305.2 110.9 %collective-permute-start.29 = (f32[4,4,1,128]{3,1,2,0:T(4,128)S(1)}, f32[4,4,1,128]{3,1,2,0:T(4,128)S(1)}, u32[]{:S(2)}, u32[]{:S(2)}) collective-permute-start(f32[4,4,1,128]{3,1,2,0:T(4,128)S(1)} %get-tuple-element.247), channel_id=1, source_target_pairs={{64,0},{128,64},{192,128},{256,192},{320,256},{384,320},{448,384},... | collective-permute-start | bytes 24584 | tf_op jit(solution)/shard_map/ppermute | solution.py:18
  416.4 7.7 %collective-permute-start.30 = (f32[4,4,18,1]{3,1,2,0:T(4,128)S(1)}, f32[4,4,18,1]{3,1,2,0:T(4,128)S(1)}, u32[]{:S(2)}, u32[]{:S(2)}) collective-permute-start(f32[4,4,18,1]{3,1,2,0:T(4,128)S(1)} %get-tuple-element.236), channel_id=1, source_target_pairs={{0,1},{1,2},{2,3},{3,4},{4,5},{5,6},{6,7},{7,8},{8,9},{9,10},{10,1... | collective-permute-start | bytes 3464 | tf_op jit(solution)/shard_map/ppermute | solution.py:15
  420.6 8.0 %collective-permute-start.31 = (f32[4,4,18,1]{3,1,2,0:T(4,128)S(1)}, f32[4,4,18,1]{3,1,2,0:T(4,128)S(1)}, u32[]{:S(2)}, u32[]{:S(2)}) collective-permute-start(f32[4,4,18,1]{3,1,2,0:T(4,128)S(1)} %get-tuple-element.237), channel_id=1, source_target_pairs={{1,0},{2,1},{3,2},{4,3},{5,4},{6,5},{7,6},{8,7},{9,8},{10,9},{11,1... | collective-permute-start | bytes 3464 | tf_op jit(solution)/shard_map/ppermute | solution.py:18
  (24 other events, 1052.4 us)
where the time goes:
time: 431 us; the launch traced here: 429 us
  blocking collectives  219 us (51%)
  starting transfers between devices  129 us (30%)
  waiting for transfers between devices  32.8 us (8%)
  other arithmetic  21.7 us (5%)
  local copies, waits for them, and re-layouts  17.1 us (4%)
  matrix products  8.29 us (2%)
    psum x1, blocking collectives, on_device(): features = lax.psum(act1.sum(axis=(2, 3)), ('face', 'tile')) / pooled_count  115 us
    psum x1, blocking collectives, on_device(): grad_f, grad_c = lax.psum((grad_f, grad_c), ('face', 'tile'))  104 us
    ppermute x16, starting transfers between devices, with_halo(): lax.ppermute(lax.slice_in_dim(block, 0, width, axis=dim), axis, backward)  82.5 us
    ppermute x16, starting transfers between devices, with_halo(): lax.ppermute(lax.slice_in_dim(block, block.shape[dim] - width, None, axis...  46.8 us
    ppermute x16, waiting for transfers between devices, with_halo(): lax.ppermute(lax.slice_in_dim(block, 0, width, axis=dim), axis, backward)  27.6 us
  transfers between devices with their start and end apart: 32, of which 13 were waited for; matrix products, arithmetic and copies ran while one was open for 4% of the time, Pallas kernels for 0%

commit v1 on v0

--- a/solution.py
+++ b/solution.py
@@ -99,7 +99,7 @@
     pre1 = jnp.einsum("kio,kbirc->borc", coarse_weight, terms1, precision=exact)
     act1 = jax.nn.softplus(pre1)
     pooled_count = nrows // 2 * lax.axis_size("face") * (ncols // 2) * lax.axis_size("tile")
-    features = lax.psum(act1.sum(axis=(2, 3)), ("face", "tile")) / pooled_count
+    features = lax.psum(lax.psum(act1.sum(axis=(2, 3)), "face"), "tile") / pooled_count
     hidden = jnp.tanh(
         jnp.dot(features, feature_weight, precision=exact)
         + jnp.dot(params, param_weight, precision=exact)

time: 431 us -> 476 us (1.10)
  blocking collectives: 219 us -> 262 us
    psum x1 -> x2, blocking collectives: 115 us -> 157 us  [the longest x1 140 us: on_device(): lax.psum(lax.psum(act1.sum(axis=(2, 3)), 'face'), 'tile') / pooled_count]
  transfers between devices with their start and end apart: 32 -> 32, of which waited for: 13 -> 12; matrix products, arithmetic and copies ran while one was open for 4% -> 3% of each run, Pallas kernels for 0% -> 0%
where the time goes in v1:
time: 476 us; the launch traced here: 475 us
  blocking collectives  262 us (55%)
  starting transfers between devices  131 us (28%)
  waiting for transfers between devices  33.2 us (7%)
  other arithmetic  21.2 us (4%)
  local copies, waits for them, and re-layouts  16.9 us (4%)
  matrix products  8.29 us (2%)
    psum x1, blocking collectives, on_device(): lax.psum(lax.psum(act1.sum(axis=(2, 3)), 'face'), 'tile') / pooled_count  140 us
    psum x1, blocking collectives, on_device(): grad_f, grad_c = lax.psum((grad_f, grad_c), ('face', 'tile'))  105 us
    ppermute x16, starting transfers between devices, with_halo(): lax.ppermute(lax.slice_in_dim(block, 0, width, axis=dim), axis, backward)  85.9 us
    ppermute x16, starting transfers between devices, with_halo(): lax.ppermute(lax.slice_in_dim(block, block.shape[dim] - width, None, axis...  45.5 us
    ppermute x16, waiting for transfers between devices, with_halo(): lax.ppermute(lax.slice_in_dim(block, 0, width, axis=dim), axis, backward)  29.5 us
    psum x1, blocking collectives, on_device(): lax.psum(act1.sum(axis=(2, 3)), 'face')  16.6 us
  transfers between devices with their start and end apart: 32, of which 12 were waited for; matrix products, arithmetic and copies ran while one was open for 3% of the time, Pallas kernels for 0%

profile of v1, /device:TPU:1, one launch (start us, length us, event | category | flops | bytes accessed | tf_op | source)
XLA Modules:
  0.0 475.0 jit_solution(2168950222777146546)
XLA Ops:
  5.6 4.1 collective-permute-start.1
  11.9 6.0 %collective-permute-start.2 = (f32[4,4,18,1]{3,1,2,0:T(4,128)S(1)}, f32[4,4,18,1]{3,1,2,0:T(4,128)S(1)}, u32[]{:S(2)}, u32[]{:S(2)}) collective-permute-start(f32[4,4,18,1]{3,1,2,0:T(4,128)S(1)} %get-tuple-element.242), channel_id=1, source_target_pairs={{0,1},{1,2},{2,3},{3,4},{4,5},{5,6},{6,7},{7,8},{8,9},{9,10},{10,1... | collective-permute-start | bytes 3464 | tf_op jit(solution)/shard_map/ppermute | solution.py:15
  18.0 4.5 collective-permute-start.3
  28.9 4.7 collective-permute-start.5
  37.5 6.9 %collective-permute-start.7 = (f32[4,4,18,1]{3,1,2,0:T(4,128)S(1)}, f32[4,4,18,1]{3,1,2,0:T(4,128)S(1)}, u32[]{:S(2)}, u32[]{:S(2)}) collective-permute-start(f32[4,4,18,1]{3,1,2,0:T(4,128)S(1)} %get-tuple-element.241), channel_id=1, source_target_pairs={{1,0},{2,1},{3,2},{4,3},{5,4},{6,5},{7,6},{8,7},{9,8},{10,9},{11,1... | collective-permute-start | bytes 3464 | tf_op jit(solution)/shard_map/ppermute | solution.py:18
  51.4 5.6 %reduce_sum.18 = f32[4,16,8,64]{1,3,2,0:T(8,128)S(1)} reduce(f32[4,16,8,2,64,2]{1,5,4,3,2,0:T(2,128)} %bitcast.121, f32[]{:T(128)} %constant.422.clone.1), dimensions={3,5}, to_apply=%region_0.1 | reduce | flops 98304 | bytes 655364 | tf_op jit(solution)/shard_map/reduce_sum | solution.py:96
  60.0 5.4 %collective-permute-start.9 = (f32[4,16,1,64]{3,1,2,0:T(8,128)S(1)}, f32[4,16,1,64]{3,1,2,0:T(8,128)S(1)}, u32[]{:S(2)}, u32[]{:S(2)}) collective-permute-start(f32[4,16,1,64]{3,1,2,0:T(8,128)S(1)} %get-tuple-element.235), channel_id=1, source_target_pairs={{64,0},{128,64},{192,128},{256,192},{320,256},{384,320},{448,384},... | collective-permute-start | bytes 49160 | tf_op jit(solution)/shard_map/ppermute | solution.py:18
  68.7 9.0 %collective-permute-start.11 = (f32[4,16,10,1]{3,1,2,0:T(8,128)S(1)}, f32[4,16,10,1]{3,1,2,0:T(8,128)S(1)}, u32[]{:S(2)}, u32[]{:S(2)}) collective-permute-start(f32[4,16,10,1]{3,1,2,0:T(8,128)S(1)} %get-tuple-element.217), channel_id=1, source_target_pairs={{1,0},{2,1},{3,2},{4,3},{5,4},{6,5},{7,6},{8,7},{9,8},{10,9},{11,1... | collective-permute-start | bytes 7688 | tf_op jit(solution)/shard_map/ppermute | solution.py:18
  81.5 6.2 %collective-permute-start.13 = (f32[4,16,1,64]{3,1,2,0:T(8,128)S(1)}, f32[4,16,1,64]{3,1,2,0:T(8,128)S(1)}, u32[]{:S(2)}, u32[]{:S(2)}) collective-permute-start(f32[4,16,1,64]{3,1,2,0:T(8,128)S(1)} %get-tuple-element.231), channel_id=1, source_target_pairs={{64,0},{128,64},{192,128},{256,192},{320,256},{384,320},{448,384},... | collective-permute-start | bytes 49160 | tf_op jit(solution)/shard_map/ppermute | solution.py:18
  90.9 11.1 %collective-permute-start.15 = (f32[4,16,10,1]{3,1,2,0:T(8,128)S(1)}, f32[4,16,10,1]{3,1,2,0:T(8,128)S(1)}, u32[]{:S(2)}, u32[]{:S(2)}) collective-permute-start(f32[4,16,10,1]{3,1,2,0:T(8,128)S(1)} %get-tuple-element.215), channel_id=1, source_target_pairs={{1,0},{2,1},{3,2},{4,3},{5,4},{6,5},{7,6},{8,7},{9,8},{10,9},{11,1... | collective-permute-start | bytes 7688 | tf_op jit(solution)/shard_map/ppermute | solution.py:18
  105.6 16.6 %psum.28 = f32[4,32]{1,0:T(4,128)S(1)} all-reduce(f32[4,32]{1,0:T(4,128)S(1)} %get-tuple-element.266), channel_id=1, replica_groups=mesh['face'=8,'tile'=64] {'face'}, use_global_device_ids=true, to_apply=%region_2.3 | all-reduce | flops 128 | bytes 1024 | tf_op jit(solution)/shard_map/psum | solution.py:102
  122.2 140.2 %psum.29 = f32[4,32]{1,0:T(4,128)S(1)} all-reduce(f32[4,32]{1,0:T(4,128)S(1)} %psum.28), channel_id=1, replica_groups=mesh['face'=8,'tile'=64] {'tile'}, use_global_device_ids=true, to_apply=%region_3.4 | all-reduce | flops 128 | bytes 1024 | tf_op jit(solution)/shard_map/psum | solution.py:102
  266.5 5.5 %collective-permute-start.17 = (f32[4,16,1,64]{3,1,2,0:T(8,128)S(1)}, f32[4,16,1,64]{3,1,2,0:T(8,128)S(1)}, u32[]{:S(2)}, u32[]{:S(2)}) collective-permute-start(f32[4,16,1,64]{3,1,2,0:T(8,128)S(1)} %get-tuple-element.225), channel_id=1, source_target_pairs={{64,0},{128,64},{192,128},{256,192},{320,256},{384,320},{448,384},... | collective-permute-start | bytes 49160 | tf_op jit(solution)/shard_map/ppermute | solution.py:18
  277.2 4.7 collective-permute-start.19
  285.1 5.9 %collective-permute-done.19 = f32[4,16,10,1]{3,1,2,0:T(8,128)S(1)} collective-permute-done((f32[4,16,10,1]{3,1,2,0:T(8,128)S(1)}, f32[4,16,10,1]{3,1,2,0:T(8,128)S(1)}, u32[]{:S(2)}, u32[]{:S(2)}) %collective-permute-start.19) | collective-permute-done | bytes 2592 | tf_op jit(solution)/shard_map/ppermute | solution.py:18
  293.2 5.7 %collective-permute-start.21 = (f32[4,16,1,64]{3,1,2,0:T(8,128)S(1)}, f32[4,16,1,64]{3,1,2,0:T(8,128)S(1)}, u32[]{:S(2)}, u32[]{:S(2)}) collective-permute-start(f32[4,16,1,64]{3,1,2,0:T(8,128)S(1)} %get-tuple-element.221), channel_id=1, source_target_pairs={{64,0},{128,64},{192,128},{256,192},{320,256},{384,320},{448,384},... | collective-permute-start | bytes 49160 | tf_op jit(solution)/shard_map/ppermute | solution.py:18
  310.3 7.0 %collective-permute-done.23 = f32[4,16,10,1]{3,1,2,0:T(8,128)S(1)} collective-permute-done((f32[4,16,10,1]{3,1,2,0:T(8,128)S(1)}, f32[4,16,10,1]{3,1,2,0:T(8,128)S(1)}, u32[]{:S(2)}, u32[]{:S(2)}) %collective-permute-start.23) | collective-permute-done | bytes 2592 | tf_op jit(solution)/shard_map/ppermute | solution.py:18
  317.9 4.0 broadcast_in_dim.2
  327.6 5.5 %collective-permute-start.25 = (f32[4,4,1,128]{3,1,2,0:T(4,128)S(1)}, f32[4,4,1,128]{3,1,2,0:T(4,128)S(1)}, u32[]{:S(2)}, u32[]{:S(2)}) collective-permute-start(f32[4,4,1,128]{3,1,2,0:T(4,128)S(1)} %get-tuple-element.251), channel_id=1, source_target_pairs={{64,0},{128,64},{192,128},{256,192},{320,256},{384,320},{448,384},... | collective-permute-start | bytes 24584 | tf_op jit(solution)/shard_map/ppermute | solution.py:18
  340.7 5.6 %collective-permute-done.27 = f32[4,4,18,1]{3,1,2,0:T(4,128)S(1)} collective-permute-done((f32[4,4,18,1]{3,1,2,0:T(4,128)S(1)}, f32[4,4,18,1]{3,1,2,0:T(4,128)S(1)}, u32[]{:S(2)}, u32[]{:S(2)}) %collective-permute-start.27) | collective-permute-done | bytes 1184 | tf_op jit(solution)/shard_map/ppermute | solution.py:18
  348.6 6.0 %collective-permute-start.29 = (f32[4,4,1,128]{3,1,2,0:T(4,128)S(1)}, f32[4,4,1,128]{3,1,2,0:T(4,128)S(1)}, u32[]{:S(2)}, u32[]{:S(2)}) collective-permute-start(f32[4,4,1,128]{3,1,2,0:T(4,128)S(1)} %get-tuple-element.247), channel_id=1, source_target_pairs={{64,0},{128,64},{192,128},{256,192},{320,256},{384,320},{448,384},... | collective-permute-start | bytes 24584 | tf_op jit(solution)/shard_map/ppermute | solution.py:18
  356.2 105.4 %all-reduce = (f32[3,4,16]{2,1,0:T(4,128)}, f32[3,16,32]{2,1,0:T(8,128)}) all-reduce(f32[3,4,16]{2,1,0:T(4,128)S(1)} %convolution_bitcast_fusion.5, f32[3,16,32]{2,1,0:T(8,128)S(1)} %convolution_bitcast_fusion.4), channel_id=1, replica_groups=mesh['face'=8,'tile'=64] {'face','tile'}, use_global_device_ids=true, to_apply=%region_4.5 | all-reduce | flops 1728 | bytes 13824 | tf_op jit(solution)/shard_map/psum | solution.py:125
  461.8 4.2 collective-permute-start.30
  469.5 4.5 collective-permute-done.31
  (170 shorter events, 89.0 us)
Async XLA Ops:
  1.6 10.2 %collective-permute-start = (f32[4,4,1,128]{3,1,2,0:T(4,128)S(1)}, f32[4,4,1,128]{3,1,2,0:T(4,128)S(1)}, u32[]{:S(2)}, u32[]{:S(2)}) collective-permute-start(f32[4,4,1,128]{3,1,2,0:T(4,128)S(1)} %get-tuple-element.258), channel_id=1, source_target_pairs={{0,64},{64,128},{128,192},{192,256},{256,320},{320,384},{384,448},... | collective-permute-start | bytes 24584 | tf_op jit(solution)/shard_map/ppermute | solution.py:15
  11.9 12.1 %collective-permute-start.2 = (f32[4,4,18,1]{3,1,2,0:T(4,128)S(1)}, f32[4,4,18,1]{3,1,2,0:T(4,128)S(1)}, u32[]{:S(2)}, u32[]{:S(2)}) collective-permute-start(f32[4,4,18,1]{3,1,2,0:T(4,128)S(1)} %get-tuple-element.242), channel_id=1, source_target_pairs={{0,1},{1,2},{2,3},{3,4},{4,5},{5,6},{6,7},{7,8},{8,9},{9,10},{10,1... | collective-permute-start | bytes 3464 | tf_op jit(solution)/shard_map/ppermute | solution.py:15
  18.0 8.0 %collective-permute-start.3 = (f32[4,4,18,1]{3,1,2,0:T(4,128)S(1)}, f32[4,4,18,1]{3,1,2,0:T(4,128)S(1)}, u32[]{:S(2)}, u32[]{:S(2)}) collective-permute-start(f32[4,4,18,1]{3,1,2,0:T(4,128)S(1)} %get-tuple-element.243), channel_id=1, source_target_pairs={{1,0},{2,1},{3,2},{4,3},{5,4},{6,5},{7,6},{8,7},{9,8},{10,9},{11,1... | collective-permute-start | bytes 3464 | tf_op jit(solution)/shard_map/ppermute | solution.py:18
  26.2 7.4 %collective-permute-start.4 = (f32[4,4,1,128]{3,1,2,0:T(4,128)S(1)}, f32[4,4,1,128]{3,1,2,0:T(4,128)S(1)}, u32[]{:S(2)}, u32[]{:S(2)}) collective-permute-start(f32[4,4,1,128]{3,1,2,0:T(4,128)S(1)} %get-tuple-element.254), channel_id=1, source_target_pairs={{0,64},{64,128},{128,192},{192,256},{256,320},{320,384},{384,448},... | collective-permute-start | bytes 24584 | tf_op jit(solution)/shard_map/ppermute | solution.py:15
  34.6 11.3 %collective-permute-start.6 = (f32[4,4,18,1]{3,1,2,0:T(4,128)S(1)}, f32[4,4,18,1]{3,1,2,0:T(4,128)S(1)}, u32[]{:S(2)}, u32[]{:S(2)}) collective-permute-start(f32[4,4,18,1]{3,1,2,0:T(4,128)S(1)} %get-tuple-element.240), channel_id=1, source_target_pairs={{0,1},{1,2},{2,3},{3,4},{4,5},{5,6},{6,7},{7,8},{8,9},{9,10},{10,1... | collective-permute-start | bytes 3464 | tf_op jit(solution)/shard_map/ppermute | solution.py:15
  37.5 8.4 %collective-permute-start.7 = (f32[4,4,18,1]{3,1,2,0:T(4,128)S(1)}, f32[4,4,18,1]{3,1,2,0:T(4,128)S(1)}, u32[]{:S(2)}, u32[]{:S(2)}) collective-permute-start(f32[4,4,18,1]{3,1,2,0:T(4,128)S(1)} %get-tuple-element.241), channel_id=1, source_target_pairs={{1,0},{2,1},{3,2},{4,3},{5,4},{6,5},{7,6},{8,7},{9,8},{10,9},{11,1... | collective-permute-start | bytes 3464 | tf_op jit(solution)/shard_map/ppermute | solution.py:18
  57.4 8.0 %collective-permute-start.8 = (f32[4,16,1,64]{3,1,2,0:T(8,128)S(1)}, f32[4,16,1,64]{3,1,2,0:T(8,128)S(1)}, u32[]{:S(2)}, u32[]{:S(2)}) collective-permute-start(f32[4,16,1,64]{3,1,2,0:T(8,128)S(1)} %get-tuple-element.234), channel_id=1, source_target_pairs={{0,64},{64,128},{128,192},{192,256},{256,320},{320,384},{384,448},... | collective-permute-start | bytes 49160 | tf_op jit(solution)/shard_map/ppermute | solution.py:15
  66.6 12.6 %collective-permute-start.10 = (f32[4,16,10,1]{3,1,2,0:T(8,128)S(1)}, f32[4,16,10,1]{3,1,2,0:T(8,128)S(1)}, u32[]{:S(2)}, u32[]{:S(2)}) collective-permute-start(f32[4,16,10,1]{3,1,2,0:T(8,128)S(1)} %get-tuple-element.216), channel_id=1, source_target_pairs={{0,1},{1,2},{2,3},{3,4},{4,5},{5,6},{6,7},{7,8},{8,9},{9,10},{10,1... | collective-permute-start | bytes 7688 | tf_op jit(solution)/shard_map/ppermute | solution.py:15
  68.7 10.5 %collective-permute-start.11 = (f32[4,16,10,1]{3,1,2,0:T(8,128)S(1)}, f32[4,16,10,1]{3,1,2,0:T(8,128)S(1)}, u32[]{:S(2)}, u32[]{:S(2)}) collective-permute-start(f32[4,16,10,1]{3,1,2,0:T(8,128)S(1)} %get-tuple-element.217), channel_id=1, source_target_pairs={{1,0},{2,1},{3,2},{4,3},{5,4},{6,5},{7,6},{8,7},{9,8},{10,9},{11,1... | collective-permute-start | bytes 7688 | tf_op jit(solution)/shard_map/ppermute | solution.py:18
  79.6 8.1 %collective-permute-start.12 = (f32[4,16,1,64]{3,1,2,0:T(8,128)S(1)}, f32[4,16,1,64]{3,1,2,0:T(8,128)S(1)}, u32[]{:S(2)}, u32[]{:S(2)}) collective-permute-start(f32[4,16,1,64]{3,1,2,0:T(8,128)S(1)} %get-tuple-element.230), channel_id=1, source_target_pairs={{0,64},{64,128},{128,192},{192,256},{256,320},{320,384},{384,448},... | collective-permute-start | bytes 49160 | tf_op jit(solution)/shard_map/ppermute | solution.py:15
  88.9 14.6 %collective-permute-start.14 = (f32[4,16,10,1]{3,1,2,0:T(8,128)S(1)}, f32[4,16,10,1]{3,1,2,0:T(8,128)S(1)}, u32[]{:S(2)}, u32[]{:S(2)}) collective-permute-start(f32[4,16,10,1]{3,1,2,0:T(8,128)S(1)} %get-tuple-element.214), channel_id=1, source_target_pairs={{0,1},{1,2},{2,3},{3,4},{4,5},{5,6},{6,7},{7,8},{8,9},{9,10},{10,1... | collective-permute-start | bytes 7688 | tf_op jit(solution)/shard_map/ppermute | solution.py:15
  90.9 12.6 %collective-permute-start.15 = (f32[4,16,10,1]{3,1,2,0:T(8,128)S(1)}, f32[4,16,10,1]{3,1,2,0:T(8,128)S(1)}, u32[]{:S(2)}, u32[]{:S(2)}) collective-permute-start(f32[4,16,10,1]{3,1,2,0:T(8,128)S(1)} %get-tuple-element.215), channel_id=1, source_target_pairs={{1,0},{2,1},{3,2},{4,3},{5,4},{6,5},{7,6},{8,7},{9,8},{10,9},{11,1... | collective-permute-start | bytes 7688 | tf_op jit(solution)/shard_map/ppermute | solution.py:18
  264.6 7.4 %collective-permute-start.16 = (f32[4,16,1,64]{3,1,2,0:T(8,128)S(1)}, f32[4,16,1,64]{3,1,2,0:T(8,128)S(1)}, u32[]{:S(2)}, u32[]{:S(2)}) collective-permute-start(f32[4,16,1,64]{3,1,2,0:T(8,128)S(1)} %get-tuple-element.224), channel_id=1, source_target_pairs={{0,64},{64,128},{128,192},{192,256},{256,320},{320,384},{384,448},... | collective-permute-start | bytes 49160 | tf_op jit(solution)/shard_map/ppermute | solution.py:15
  273.9 11.1 %collective-permute-start.18 = (f32[4,16,10,1]{3,1,2,0:T(8,128)}, f32[4,16,10,1]{3,1,2,0:T(8,128)S(1)}, u32[]{:S(2)}, u32[]{:S(2)}) collective-permute-start(f32[4,16,10,1]{3,1,2,0:T(8,128)} %get-tuple-element.212), channel_id=1, source_target_pairs={{0,1},{1,2},{2,3},{3,4},{4,5},{5,6},{6,7},{7,8},{8,9},{9,10},{10,1... | collective-permute-start | bytes 7688 | tf_op jit(solution)/shard_map/ppermute | solution.py:15
  277.2 13.8 %collective-permute-start.19 = (f32[4,16,10,1]{3,1,2,0:T(8,128)S(1)}, f32[4,16,10,1]{3,1,2,0:T(8,128)S(1)}, u32[]{:S(2)}, u32[]{:S(2)}) collective-permute-start(f32[4,16,10,1]{3,1,2,0:T(8,128)S(1)} %get-tuple-element.213), channel_id=1, source_target_pairs={{1,0},{2,1},{3,2},{4,3},{5,4},{6,5},{7,6},{8,7},{9,8},{10,9},{11,1... | collective-permute-start | bytes 7688 | tf_op jit(solution)/shard_map/ppermute | solution.py:18
  291.3 7.6 %collective-permute-start.20 = (f32[4,16,1,64]{3,1,2,0:T(8,128)S(1)}, f32[4,16,1,64]{3,1,2,0:T(8,128)S(1)}, u32[]{:S(2)}, u32[]{:S(2)}) collective-permute-start(f32[4,16,1,64]{3,1,2,0:T(8,128)S(1)} %get-tuple-element.220), channel_id=1, source_target_pairs={{0,64},{64,128},{128,192},{192,256},{256,320},{320,384},{384,448},... | collective-permute-start | bytes 49160 | tf_op jit(solution)/shard_map/ppermute | solution.py:15
  300.6 9.6 %collective-permute-start.22 = (f32[4,16,10,1]{3,1,2,0:T(8,128)}, f32[4,16,10,1]{3,1,2,0:T(8,128)S(1)}, u32[]{:S(2)}, u32[]{:S(2)}) collective-permute-start(f32[4,16,10,1]{3,1,2,0:T(8,128)} %get-tuple-element.210), channel_id=1, source_target_pairs={{0,1},{1,2},{2,3},{3,4},{4,5},{5,6},{6,7},{7,8},{8,9},{9,10},{10,1... | collective-permute-start | bytes 7688 | tf_op jit(solution)/shard_map/ppermute | solution.py:15
  303.8 13.4 %collective-permute-start.23 = (f32[4,16,10,1]{3,1,2,0:T(8,128)S(1)}, f32[4,16,10,1]{3,1,2,0:T(8,128)S(1)}, u32[]{:S(2)}, u32[]{:S(2)}) collective-permute-start(f32[4,16,10,1]{3,1,2,0:T(8,128)S(1)} %get-tuple-element.211), channel_id=1, source_target_pairs={{1,0},{2,1},{3,2},{4,3},{5,4},{6,5},{7,6},{8,7},{9,8},{10,9},{11,1... | collective-permute-start | bytes 7688 | tf_op jit(solution)/shard_map/ppermute | solution.py:18
  325.7 8.3 %collective-permute-start.24 = (f32[4,4,1,128]{3,1,2,0:T(4,128)S(1)}, f32[4,4,1,128]{3,1,2,0:T(4,128)S(1)}, u32[]{:S(2)}, u32[]{:S(2)}) collective-permute-start(f32[4,4,1,128]{3,1,2,0:T(4,128)S(1)} %get-tuple-element.250), channel_id=1, source_target_pairs={{0,64},{64,128},{128,192},{192,256},{256,320},{320,384},{384,448},... | collective-permute-start | bytes 24584 | tf_op jit(solution)/shard_map/ppermute | solution.py:15
  337.3 9.1 %collective-permute-start.27 = (f32[4,4,18,1]{3,1,2,0:T(4,128)S(1)}, f32[4,4,18,1]{3,1,2,0:T(4,128)S(1)}, u32[]{:S(2)}, u32[]{:S(2)}) collective-permute-start(f32[4,4,18,1]{3,1,2,0:T(4,128)S(1)} %get-tuple-element.239), channel_id=1, source_target_pairs={{1,0},{2,1},{3,2},{4,3},{5,4},{6,5},{7,6},{8,7},{9,8},{10,9},{11,1... | collective-permute-start | bytes 3464 | tf_op jit(solution)/shard_map/ppermute | solution.py:18
  346.6 115.0 %collective-permute-start.28 = (f32[4,4,1,128]{3,1,2,0:T(4,128)S(1)}, f32[4,4,1,128]{3,1,2,0:T(4,128)S(1)}, u32[]{:S(2)}, u32[]{:S(2)}) collective-permute-start(f32[4,4,1,128]{3,1,2,0:T(4,128)S(1)} %get-tuple-element.246), channel_id=1, source_target_pairs={{0,64},{64,128},{128,192},{192,256},{256,320},{320,384},{384,448},... | collective-permute-start | bytes 24584 | tf_op jit(solution)/shard_map/ppermute | solution.py:15
  348.6 113.1 %collective-permute-start.29 = (f32[4,4,1,128]{3,1,2,0:T(4,128)S(1)}, f32[4,4,1,128]{3,1,2,0:T(4,128)S(1)}, u32[]{:S(2)}, u32[]{:S(2)}) collective-permute-start(f32[4,4,1,128]{3,1,2,0:T(4,128)S(1)} %get-tuple-element.247), channel_id=1, source_target_pairs={{64,0},{128,64},{192,128},{256,192},{320,256},{384,320},{448,384},... | collective-permute-start | bytes 24584 | tf_op jit(solution)/shard_map/ppermute | solution.py:18
  461.8 7.7 %collective-permute-start.30 = (f32[4,4,18,1]{3,1,2,0:T(4,128)S(1)}, f32[4,4,18,1]{3,1,2,0:T(4,128)S(1)}, u32[]{:S(2)}, u32[]{:S(2)}) collective-permute-start(f32[4,4,18,1]{3,1,2,0:T(4,128)S(1)} %get-tuple-element.236), channel_id=1, source_target_pairs={{0,1},{1,2},{2,3},{3,4},{4,5},{5,6},{6,7},{7,8},{8,9},{9,10},{10,1... | collective-permute-start | bytes 3464 | tf_op jit(solution)/shard_map/ppermute | solution.py:15
  466.1 8.0 %collective-permute-start.31 = (f32[4,4,18,1]{3,1,2,0:T(4,128)S(1)}, f32[4,4,18,1]{3,1,2,0:T(4,128)S(1)}, u32[]{:S(2)}, u32[]{:S(2)}) collective-permute-start(f32[4,4,18,1]{3,1,2,0:T(4,128)S(1)} %get-tuple-element.237), channel_id=1, source_target_pairs={{1,0},{2,1},{3,2},{4,3},{5,4},{6,5},{7,6},{8,7},{9,8},{10,9},{11,1... | collective-permute-start | bytes 3464 | tf_op jit(solution)/shard_map/ppermute | solution.py:18
  (24 other events, 1262.2 us)
